TPU v7x, 512 devices: a whole 4x4x16 slice. The times are simulated.
512 devices in a mesh: cls: 32 (over z, core), pen: 16 (over x, y).
Axes of the slice: x: 4, y: 4, z: 16, core: 2. Of those that a mesh axis runs over, the one named last changes fastest.
Arguments:
- fourier_slabs: bfloat16 [32768, 128, 128], P(('cls', 'pen')), may hold values from -6 to 6
- class_id: int32 [32768, 1], P(('cls', 'pen')), may hold values from 0 to 63; in each aligned block of 64 rows (0 to 63, 64 to 127, ...) at most 2 rows name the same one
- orientation: int32 [32768], P(('cls', 'pen')), may hold values from 0 to 127
- offset: bfloat16 [32768], P(('cls', 'pen')), may hold values from 0.099609375 to 0.8984375
- tomogram: int32 [32768], P(('cls', 'pen')), may hold values from 0 to 255
- defocus: bfloat16 [256], replicated, may hold values from 1 to 4
- class_map: bfloat16 [64, 128, 128, 128], P('cls', None, 'pen'), may hold values from -6 to 6
Outputs:
- class_gradient: float32 [64, 128, 128, 128], P('cls', 'pen')
Inputs may be any that keep to these rules, and one draw needn't show every extreme that they name: `class_id`: in each aligned block of 64 rows (the particles of one device) no class is named by more than 2 rows, a bound that some block reaches.
All inputs are finite; a program needn't handle non-finite values.
Results may differ from a plain program's by a relative error of at most 0.0029.
Values may be sent and summed in bfloat16 or wider, within the bound.
A program may use at most 64 MiB of HBM per device.

v0:
```python
import math

import jax
import jax.numpy as jnp
from jax import lax
from jax.sharding import PartitionSpec as P

AMPLITUDE = 0.07
HIGHEST = lax.Precision.HIGHEST


def frequency(indices, extent):
    return jnp.where(indices < extent // 2, indices, indices - extent).astype(jnp.float32)


def hartley_table(extent):
    indices = jnp.arange(extent, dtype=jnp.int32)
    product = jnp.mod(indices[:, None] * indices[None, :], extent).astype(jnp.float32)
    angles = 2.0 * math.pi / extent * product
    return (jnp.cos(angles) + jnp.sin(angles)) / math.sqrt(extent)


def interp_kernel(position, extent):
    planes = jnp.arange(extent, dtype=jnp.float32)
    spacing = planes[:, None] - position[None, :]
    return (
        jnp.sin(math.pi * spacing)
        * jnp.cos(math.pi * spacing / extent)
        / (extent * jnp.sin(math.pi * spacing / extent))
    )


def contrast(focus_slot, shell_sq):
    phase_angle = math.pi * focus_slot[:, None] * shell_sq[None, :]
    return -(
        math.sqrt(1.0 - AMPLITUDE * AMPLITUDE) * jnp.sin(phase_angle)
        + AMPLITUDE * jnp.cos(phase_angle)
    )


def per_device(fourier_slabs, class_id, orientation, offset, tomogram, defocus, class_map):
    particles_here, extent_y, extent_z = fourier_slabs.shape
    local_classes, extent_x = (class_map.shape[0], class_map.shape[1])
    owner_count = lax.axis_size("cls")
    pencil_count = lax.axis_size("pen")
    classes = local_classes * owner_count
    capacity = max(2, 2 * particles_here // classes)
    rows_local = extent_y // pencil_count
    voxels_local = rows_local * extent_z
    class_ids = class_id[:, 0]
    labels = jnp.arange(classes, dtype=jnp.int32)
    member = (class_ids[:, None] == labels[None, :]).astype(jnp.int32)
    earlier = jnp.cumsum(member, axis=0) - member
    order_in = jnp.sum(earlier * member, axis=1)
    slot_index = class_ids * capacity + order_in
    targets = jnp.arange(classes * capacity, dtype=jnp.int32)
    dispatch = (targets[:, None] == slot_index[None, :]).astype(jnp.bfloat16)
    flat_slabs = fourier_slabs.reshape(particles_here, extent_y * extent_z)
    packed = jnp.dot(dispatch, flat_slabs, preferred_element_type=jnp.float32).astype(jnp.bfloat16)
    tomo_match = tomogram[:, None] == jnp.arange(defocus.shape[0], dtype=jnp.int32)[None, :]
    focus_here = jnp.sum(jnp.where(tomo_match, defocus.astype(jnp.float32)[None, :], 0.0), axis=1)
    fields = jnp.stack(
        [
            orientation.astype(jnp.float32),
            offset.astype(jnp.float32),
            focus_here,
            jnp.ones((particles_here,), jnp.float32),
        ],
        axis=1,
    ).astype(jnp.bfloat16)
    slot_labels = jnp.dot(dispatch, fields, preferred_element_type=jnp.float32).astype(jnp.bfloat16)
    per_owner = local_classes * capacity
    send_slabs = packed.reshape(owner_count, per_owner, extent_y, extent_z)
    send_labels = jnp.broadcast_to(
        slot_labels.reshape(owner_count, per_owner, 1, 4), (owner_count, per_owner, pencil_count, 4)
    )
    got_slabs, got_labels = (
        lax.all_to_all(
            lax.all_to_all(send_slabs, "cls", split_axis=0, concat_axis=1, tiled=True),
            "pen",
            split_axis=2,
            concat_axis=1,
            tiled=True,
        ),
        lax.all_to_all(
            lax.all_to_all(send_labels, "cls", split_axis=0, concat_axis=1, tiled=True),
            "pen",
            split_axis=2,
            concat_axis=1,
            tiled=True,
        ),
    )
    senders = got_slabs.shape[1] // per_owner
    arrived = got_slabs.reshape(senders, local_classes, capacity, voxels_local)
    labels_in = got_labels.reshape(senders, local_classes, capacity, 4).astype(jnp.float32)
    start_row = lax.axis_index("pen") * rows_local
    rows_freq = frequency(start_row + jnp.arange(rows_local, dtype=jnp.int32), extent_y)
    cols_freq = frequency(jnp.arange(extent_z, dtype=jnp.int32), extent_z)
    shell_sq = (
        ((2.0 * rows_freq / extent_y) ** 2)[:, None] + ((2.0 * cols_freq / extent_z) ** 2)[None, :]
    ).reshape(voxels_local)
    results = []
    for member_class in range(local_classes):
        slot_info = labels_in[:, member_class].reshape(senders * capacity, 4)
        valid = slot_info[:, 3]
        position = slot_info[:, 0] + slot_info[:, 1] + 0.5 * (1.0 - valid)
        kernel = interp_kernel(position, extent_x).astype(jnp.bfloat16)
        volume = class_map[member_class].reshape(extent_x, voxels_local)
        predicted = lax.dot_general(
            kernel, volume, (((0,), (0,)), ((), ())), preferred_element_type=jnp.float32
        )
        contrast_map = contrast(slot_info[:, 2], shell_sq)
        slab_rows = arrived[:, member_class].reshape(senders * capacity, voxels_local)
        weighted = (valid[:, None] * contrast_map * (slab_rows - contrast_map * predicted)).astype(
            jnp.bfloat16
        )
        results.append(jnp.dot(kernel, weighted, preferred_element_type=jnp.float32))
    gradient = jnp.stack(results).reshape(local_classes, extent_x, rows_local, extent_z)
    along_z = jnp.einsum("cxyz,zk->cxyk", gradient, hartley_table(extent_z), precision=HIGHEST)
    along_x = jnp.einsum("kx,cxyz->ckyz", hartley_table(extent_x), along_z, precision=HIGHEST)
    table_y = hartley_table(extent_y)
    return jnp.einsum(
        "ky,cxyz->cxkz",
        table_y,
        lax.all_to_all(along_x, "pen", split_axis=1, concat_axis=2, tiled=True),
        precision=HIGHEST,
    )


def solution(mesh):
    in_specs = (
        P(("cls", "pen"), None, None),
        P(("cls", "pen"), None),
        P(("cls", "pen")),
        P(("cls", "pen")),
        P(("cls", "pen")),
        P(),
        P("cls", None, "pen", None),
    )
    out_specs = P("cls", "pen", None, None)
    return jax.shard_map(
        per_device, mesh=mesh, in_specs=in_specs, out_specs=out_specs, check_vma=False
    )
```

profile of v0, /device:TPU:1, one launch (start us, length us, event | category | flops | bytes accessed | tf_op | source)
XLA Modules:
  0.0 414.9 jit_solution(5801930281145544722)
XLA Ops:
  6.5 16.7 %all-to-all-start = ((bf16[32,2,128]{2,1,0:T(2,128)(2,1)}), bf16[32,2,128]{2,1,0:T(2,128)(2,1)S(1)}, u32[]{:S(2)}, u32[]{:S(2)}) async-start(bf16[32,2,128]{2,1,0:T(2,128)(2,1)} %reshape.121), calls=%async_computation | async-start | bytes 32768 | tf_op jit(solution)/shard_map/all_to_all | solution.py:86
  23.2 3.3 fusion.18
  26.6 3.2 copy.99
  29.8 5.2 %all-to-all-done = bf16[32,2,128]{2,1,0:T(2,128)(2,1)S(1)} async-done(((bf16[32,2,128]{2,1,0:T(2,128)(2,1)}), bf16[32,2,128]{2,1,0:T(2,128)(2,1)S(1)}, u32[]{:S(2)}, u32[]{:S(2)}) %all-to-all-start) | async-done | bytes 16416 | tf_op jit(solution)/shard_map/all_to_all | solution.py:86
  35.0 7.1 %all-to-all-start.2 = ((bf16[32,4,128,128]{3,2,1,0:T(8,128)(2,1)}), bf16[32,4,128,128]{3,2,1,0:T(8,128)(2,1)}, u32[]{:S(2)}, u32[]{:S(2)}) async-start(bf16[32,4,128,128]{3,2,1,0:T(8,128)(2,1)} %bitcast.99), calls=%async_computation.2 | async-start | bytes 8388608 | tf_op jit(solution)/shard_map/all_to_all | solution.py:79
  42.9 182.4 %all-to-all-done.2 = bf16[32,4,128,128]{3,2,1,0:T(8,128)(2,1)} async-done(((bf16[32,4,128,128]{3,2,1,0:T(8,128)(2,1)}), bf16[32,4,128,128]{3,2,1,0:T(8,128)(2,1)}, u32[]{:S(2)}, u32[]{:S(2)}) %all-to-all-start.2) | async-done | bytes 4194336 | tf_op jit(solution)/shard_map/all_to_all | solution.py:79
  225.3 6.8 %all-to-all-start.1 = ((bf16[1,128,16,4]{1,3,0,2:T(4,128)(2,1)}), bf16[1,128,16,4]{1,3,0,2:T(4,128)(2,1)S(1)}, u32[]{:S(2)}, u32[]{:S(2)}) async-start(bf16[1,128,16,4]{1,3,0,2:T(4,128)(2,1)} %copy.64), calls=%async_computation.1 | async-start | bytes 32768 | tf_op jit(solution)/shard_map/all_to_all | solution.py:85
  232.1 7.4 %copy.70 = bf16[32,4,128,128]{3,1,0,2:T(4,128)(2,1)} copy(bf16[32,4,128,128]{3,2,1,0:T(8,128)(2,1)} %all-to-all-done.2) | data formatting | bytes 8388608 | tf_op jit(solution)/shard_map/all_to_all | solution.py:79
  239.5 7.1 %all-to-all-start.3 = ((bf16[1,128,128,128]{3,1,0,2:T(8,128)(2,1)}), bf16[1,128,128,128]{3,1,0,2:T(8,128)(2,1)}, u32[]{:S(2)}, u32[]{:S(2)}) async-start(bf16[1,128,128,128]{3,1,0,2:T(8,128)(2,1)} %bitcast.98), calls=%async_computation.3 | async-start | bytes 8388608 | tf_op jit(solution)/shard_map/all_to_all | solution.py:78
  250.1 3.8 divide_convert_fusion.19
  253.9 3.8 divide_convert_fusion.18
  257.7 42.3 %all-to-all-done.3 = bf16[1,128,128,128]{3,1,0,2:T(8,128)(2,1)} async-done(((bf16[1,128,128,128]{3,1,0,2:T(8,128)(2,1)}), bf16[1,128,128,128]{3,1,0,2:T(8,128)(2,1)}, u32[]{:S(2)}, u32[]{:S(2)}) %all-to-all-start.3) | async-done | bytes 4194336 | tf_op jit(solution)/shard_map/all_to_all | solution.py:78
  300.1 4.9 %copy.131 = bf16[1,128,128,128]{3,2,1,0:T(8,128)(2,1)S(1)} copy(bf16[1,128,128,128]{3,1,0,2:T(8,128)(2,1)} %all-to-all-done.3) | data formatting | bytes 8388608 | tf_op jit(solution)/shard_map/all_to_all | solution.py:78
  304.9 3.0 copy.72
  308.0 7.0 %reshape.114 = bf16[512,2,2,1024]{3,2,1,0:T(2,128)(2,1)} reshape(bf16[1,16,128,8,128]{4,3,2,1,0:T(8,128)(2,1)} %copy.72) | data formatting | bytes 8388608 | tf_op jit(solution)/shard_map/reshape | solution.py:94
  314.9 8.4 %slice_convert_fusion.1 = (f32[512,1,2,1024]{3,2,1,0:T(2,128)}, f32[512,1,2,1024]{3,2,1,0:T(2,128)}) fusion(bf16[512,2,2,1024]{3,2,1,0:T(2,128)(2,1)} %reshape.114), kind=kLoop, calls=%fused_computation.28 | loop fusion | flops 2097152 | bytes 12582912 | tf_op jit(solution)/shard_map/convert_element_type | solution.py:114
  323.3 6.6 %reshape.117 = f32[1024,1024]{1,0:T(8,128)} reshape(f32[512,1,2,1024]{3,2,1,0:T(2,128)} %get-tuple-element.6) | data formatting | bytes 8388608 | tf_op jit(solution)/shard_map/convert_element_type | solution.py:114
  329.9 22.4 %fusion.24 = f32[16,8,8,128]{3,1,2,0:T(8,128)S(1)} fusion(f32[1024,1024]{1,0:T(8,128)} %reshape.117, f32[1024]{0:T(1024)S(1)} %bitcast.118, f32[1024]{0:T(1024)S(1)} %bitcast.113, f32[1024]{0:T(1024)S(1)} %add_bitcast_fusion, bf16[16,8,8,128]{3,2,1,0:T(8,128)(2,1)S(1)} %bitcast.110, f32[1024]{0:T(1024)S(1)} %multiply_add_fusion, ...), kind=kOutput, calls=%fused_computation.34 | convolution fusion | flops 548274176 | bytes 5259264 | tf_op jit(solution)/shard_map/dot_general | solution.py:117
  352.5 6.3 %reshape.116 = f32[1024,1024]{1,0:T(8,128)} reshape(f32[512,1,2,1024]{3,2,1,0:T(2,128)} %get-tuple-element.5) | data formatting | bytes 8388608 | tf_op jit(solution)/shard_map/convert_element_type | solution.py:114
  358.8 22.6 %fusion.23 = f32[16,8,8,128]{3,1,2,0:T(8,128)S(1)} fusion(f32[1024,1024]{1,0:T(8,128)} %reshape.116, f32[1024]{0:T(1024)S(1)} %add_bitcast_fusion, f32[1024]{0:T(1024)S(1)} %bitcast.119, f32[1024]{0:T(1024)S(1)} %bitcast.115, bf16[16,8,8,128]{3,2,1,0:T(8,128)(2,1)S(1)} %bitcast.109, f32[1024]{0:T(1024)S(1)} %multiply_add_fusion.1, ...), kind=kOutput, calls=%fused_computation.33 | convolution fusion | flops 548274176 | bytes 5259264 | tf_op jit(solution)/shard_map/dot_general | solution.py:117
  381.6 1.3 fusion.25
  384.9 26.5 %all_to_all.66 = f32[2,128,8,128]{3,2,0,1:T(8,128)S(1)} all-to-all(f32[2,128,8,128]{3,2,0,1:T(8,128)S(1)} %copy.80), channel_id=1, replica_groups=mesh['cls'=32,'pen'=16] {'pen'}, dimensions={1} | all-to-all | bytes 2097152 | tf_op jit(solution)/shard_map/all_to_all | solution.py:125
  411.4 1.9 convolution_bitcast_fusion
  413.4 1.3 copy.84
  (44 shorter events, 13.0 us)
Async XLA Ops:
  6.5 28.5 %all-to-all-start = ((bf16[32,2,128]{2,1,0:T(2,128)(2,1)}), bf16[32,2,128]{2,1,0:T(2,128)(2,1)S(1)}, u32[]{:S(2)}, u32[]{:S(2)}) async-start(bf16[32,2,128]{2,1,0:T(2,128)(2,1)} %reshape.121), calls=%async_computation | async-start | bytes 32768 | tf_op jit(solution)/shard_map/all_to_all | solution.py:86
  35.0 190.3 %all-to-all-start.2 = ((bf16[32,4,128,128]{3,2,1,0:T(8,128)(2,1)}), bf16[32,4,128,128]{3,2,1,0:T(8,128)(2,1)}, u32[]{:S(2)}, u32[]{:S(2)}) async-start(bf16[32,4,128,128]{3,2,1,0:T(8,128)(2,1)} %bitcast.99), calls=%async_computation.2 | async-start | bytes 8388608 | tf_op jit(solution)/shard_map/all_to_all | solution.py:79
  225.3 14.2 %all-to-all-start.1 = ((bf16[1,128,16,4]{1,3,0,2:T(4,128)(2,1)}), bf16[1,128,16,4]{1,3,0,2:T(4,128)(2,1)S(1)}, u32[]{:S(2)}, u32[]{:S(2)}) async-start(bf16[1,128,16,4]{1,3,0,2:T(4,128)(2,1)} %copy.64), calls=%async_computation.1 | async-start | bytes 32768 | tf_op jit(solution)/shard_map/all_to_all | solution.py:85
  239.5 7.3 %copy-start = (bf16[2,128,8,128]{3,2,1,0:T(8,128)(2,1)S(1)}, bf16[2,128,8,128]{3,2,1,0:T(8,128)(2,1)}, u32[]{:S(2)}) copy-start(bf16[2,128,8,128]{3,2,1,0:T(8,128)(2,1)} %param.13) | copy-start | bytes 1572868
  239.5 60.6 %all-to-all-start.3 = ((bf16[1,128,128,128]{3,1,0,2:T(8,128)(2,1)}), bf16[1,128,128,128]{3,1,0,2:T(8,128)(2,1)}, u32[]{:S(2)}, u32[]{:S(2)}) async-start(bf16[1,128,128,128]{3,1,0,2:T(8,128)(2,1)} %bitcast.98), calls=%async_computation.3 | async-start | bytes 8388608 | tf_op jit(solution)/shard_map/all_to_all | solution.py:78
where the time goes:
time: 423 us; the launch traced here: 415 us
  waiting for transfers between devices  230 us (54%)
  matrix products  53.7 us (13%)
  local copies, waits for them, and re-layouts  45 us (11%)
  starting transfers between devices  37.7 us (9%)
  blocking collectives  26.5 us (6%)
  other arithmetic  21.6 us (5%)
    all_to_all x1, waiting for transfers between devices, per_device(): lax.all_to_all(send_slabs, 'cls', split_axis=0, concat_axis=1, tiled=True)  182 us
    dot_general x2, matrix products, per_device(): jnp.dot(kernel, weighted, preferred_element_type=jnp.float32)  45 us
    all_to_all x1, waiting for transfers between devices, per_device(): lax.all_to_all(lax.all_to_all(send_slabs, 'cls', split_axis=0, concat_axi...  42.3 us
    all_to_all x1, blocking collectives, per_device(): lax.all_to_all(along_x, 'pen', split_axis=1, concat_axis=2, tiled=True)  26.5 us
    all_to_all x1, starting transfers between devices, per_device(): lax.all_to_all(send_labels, 'cls', split_axis=0, concat_axis=1, tiled=True)  16.7 us
    convert_element_type x2, local copies, waits for them, and re-layouts, per_device(): slab_rows - contrast_map * predicted  12.9 us
  transfers between devices with their start and end apart: 4, of which 3 were waited for; matrix products, arithmetic and copies ran while one was open for 6% of the time, Pallas kernels for 0%

commit v1 on v0

v1 whole, which is shorter than its diff:
```python
import functools
import math

import jax
import jax.numpy as jnp
import numpy as np
from jax import lax
from jax.experimental import pallas as pl
from jax.experimental.pallas import tpu as pltpu
from jax.sharding import PartitionSpec as P

AMPLITUDE = 0.07
MESH = pl.DeviceIdType.MESH
F32 = jnp.float32
BF16 = jnp.bfloat16

EXTENT = 128
ZC = 16
PENS = 16
PART = 64
PLANE = PART * PENS
CHUNKS = 4
WIDE = 2 * EXTENT
POOL = 128
MAIN = 96


def power_series(function, degree, reach):
    nodes = np.cos(np.pi * (np.arange(degree + 1) + 0.5) / (degree + 1))
    nodes = 0.5 * reach * (nodes + 1.0)
    return [float(c) for c in np.polyfit(nodes, function(nodes), degree)[::-1]]


SIN_TURN = power_series(lambda s: 2 * np.pi * np.sinc(2 * np.sqrt(s)), 6, 0.25)
SIN_HALF = power_series(lambda s: np.pi * np.sinc(np.sqrt(s)), 5, 0.25)
COS_HALF = power_series(lambda s: np.cos(np.pi * np.sqrt(s)), 5, 0.25)
PHASE = math.asin(AMPLITUDE) / (2 * math.pi)


def horner(coefficients, x):
    total = coefficients[-1]
    for c in coefficients[-2::-1]:
        total = total * x + c
    return total


def hartley_tables():
    k = np.arange(EXTENT)
    angles = 2.0 * np.pi / EXTENT * ((k[:, None] * k[None, :]) % EXTENT)
    table = ((np.cos(angles) + np.sin(angles)) / math.sqrt(EXTENT)).astype(np.float32)
    high = table.astype(jnp.bfloat16)
    low = (table - high.astype(np.float32)).astype(jnp.bfloat16)
    return (
        np.concatenate([high, high, low], 0),
        np.concatenate([high, high, low], 1),
        np.concatenate([high, low], 1),
    )


def iota(shape, dim):
    return lax.broadcasted_iota(jnp.int32, shape, dim)


def dot(a, b):
    return jnp.dot(a, b, preferred_element_type=F32)


def dot_nt(a, b):
    return lax.dot_general(a, b, (((1,), (1,)), ((), ())), preferred_element_type=F32)


def split(a):
    high = a.astype(BF16)
    return high, (a - high.astype(F32)).astype(BF16)


def round_kernel(
    slots, first,
    lab_ref, slabs_ref, maps_ref, hz_ref, hx_ref, hy_ref,
    out_ref, most_ref,
    labp, p1, disp, labs, labr, send, recv, volume, kern, kern_t, focus, weighted,
    partial, partner, fs, fr, gather, flag_s, flag_r,
    lp_s, lp_r, p1_s, p1_r, own_s, cm_s, cm_r, cm_o, zl_s, zl_r, z_s, z_r, fl_s, fl_r, c_s, c_r, f_s, f_r,
):
    me = lax.axis_index("cls")
    pen = lax.axis_index("pen")
    z = me // 2
    core = lax.rem(me, 2)
    twin = (z * 2 + 1 - core, pen)

    def pen_at(o):
        return lax.rem(pen + o, PENS)

    def pen_from(o):
        return lax.rem(pen - o + PENS, PENS)

    def chip_at(o):
        return lax.rem(z + o, ZC)

    def chip_from(o):
        return lax.rem(z - o + ZC, ZC)

    def remote(src, dst, s, r, device):
        return pltpu.make_async_remote_copy(
            src_ref=src, dst_ref=dst, send_sem=s, recv_sem=r, device_id=device, device_id_type=MESH
        )

    def each(body, low=1, high=16):
        def step(i, carry):
            body(i)
            return carry

        lax.fori_loop(low, high, step, 0)

    barrier = pltpu.get_barrier_semaphore()

    def greet(o):
        pl.semaphore_signal(barrier, inc=1, device_id=(me, pen_at(o)), device_id_type=MESH)
        pl.semaphore_signal(barrier, inc=1, device_id=(chip_at(o) * 2 + core, pen), device_id_type=MESH)

    each(greet)
    pl.semaphore_signal(barrier, inc=1, device_id=twin, device_id_type=MESH)
    pl.semaphore_wait(barrier, 31)

    def lab_out(o):
        return remote(lab_ref, labp.at[pen], lp_s.at[o], lp_r.at[o], (me, pen_at(o)))

    def lab_in(o):
        return remote(lab_ref, labp.at[pen_from(o)], lp_s.at[o], lp_r.at[o], (me, pen_at(o)))

    def rows_out(j, o):
        to = pen_at(o)
        return remote(slabs_ref.at[to * CHUNKS + j], p1.at[j, pen], p1_s.at[j, o], p1_r.at[j, o], (me, to))

    def rows_in(j, o):
        to = pen_at(o)
        return remote(slabs_ref.at[to * CHUNKS + j], p1.at[j, pen_from(o)], p1_s.at[j, o], p1_r.at[j, o], (me, to))

    def rows_own(j):
        return pltpu.make_async_copy(slabs_ref.at[pen * CHUNKS + j], p1.at[j, pen], own_s.at[j])

    def map_out():
        return remote(maps_ref, volume.at[:, pl.ds(2 * core, 2)], cm_s, cm_r, twin)

    def map_in():
        return remote(maps_ref, volume.at[:, pl.ds(2 - 2 * core, 2)], cm_s, cm_r, twin)

    def map_own():
        return pltpu.make_async_copy(maps_ref, volume.at[:, pl.ds(2 * core, 2)], cm_o)

    def zlab_out(o):
        to = chip_at(o)
        return remote(labs.at[to], labr.at[z], zl_s.at[o], zl_r.at[o], (to * 2 + core, pen))

    def zlab_in(o):
        to = chip_at(o)
        return remote(labs.at[to], labr.at[chip_from(o)], zl_s.at[o], zl_r.at[o], (to * 2 + core, pen))

    def slot_out(j, o):
        to = chip_at(o)
        return remote(send.at[j, to], recv.at[j, z], z_s.at[j, o], z_r.at[j, o], (to * 2 + core, pen))

    def slot_in(j, o):
        to = chip_at(o)
        return remote(send.at[j, to], recv.at[j, chip_from(o)], z_s.at[j, o], z_r.at[j, o], (to * 2 + core, pen))

    def flag_copy():
        return remote(flag_s, flag_r, fl_s, fl_r, twin)

    def half_copy(j):
        return remote(partial.at[j, 1 - core], partner.at[j], c_s.at[j], c_r.at[j], twin)

    def cells_out(j, o):
        to = pen_at(o)
        return remote(fs.at[j, to], fr.at[j, pen], f_s.at[j, o], f_r.at[j, o], (me, to))

    def cells_in(j, o):
        to = pen_at(o)
        return remote(fs.at[j, to], fr.at[j, pen_from(o)], f_s.at[j, o], f_r.at[j, o], (me, to))

    each(lambda o: lab_out(o).start())
    for j in range(CHUNKS):
        each(lambda o, j=j: rows_out(j, o).start())
        rows_own(j).start()
    map_out().start()
    map_own().start()
    labp[pen] = lab_ref[...]
    labs[...] = jnp.zeros_like(labs)
    weighted[...] = jnp.zeros_like(weighted)

    each(lambda o: lab_in(o).wait_recv())
    fields = jnp.concatenate(
        [labp[2 * i].astype(F32) + labp[2 * i + 1].astype(F32) for i in range(PENS // 2)], axis=1
    )
    ids = fields[0:1]
    chip = jnp.floor(ids * 0.25)
    local = ids - 4.0 * chip + 1.0
    tri = jnp.where(iota((128, 128), 0) < iota((128, 128), 1), 1.0, 0.0).astype(BF16)
    running = jnp.zeros((ZC, 1), F32)
    ranks = []
    for i in range(PLANE // 128):
        part = chip[:, i * 128 : (i + 1) * 128]
        hot = jnp.where(iota((ZC, 128), 0).astype(F32) == part, 1.0, 0.0)
        before = dot(hot.astype(BF16), tri) + running
        ranks.append(jnp.sum(hot * before, axis=0, keepdims=True))
        running = running + jnp.sum(hot, axis=1, keepdims=True)
    most = jnp.max(running, axis=0, keepdims=True)
    rank = jnp.concatenate(ranks, axis=1) - float(first)
    rank = jnp.where((rank >= 0.0) & (rank < float(slots)), rank, -1.0)
    described = jnp.where(iota((16, PLANE), 0) == 0, local, fields).astype(BF16)
    row_of = iota((slots, PLANE), 0).astype(F32)

    def assign(d):
        here = jnp.where(chip == d.astype(F32), rank, -1.0)
        table = jnp.where(row_of == here, 1.0, 0.0).astype(BF16)
        disp[d] = table
        told = dot_nt(described, table)
        labs[d, :, 0:slots] = jnp.where(iota((16, slots), 0) == 4, most, told).astype(BF16)

    each(assign, 0, ZC)
    each(lambda o: zlab_out(o).start())
    labr[z] = labs[z]

    for j in range(CHUNKS):
        each(lambda o, j=j: rows_in(j, o).wait_recv())
        rows_own(j).wait()

        def pack(g, j=j):
            lines = p1[j].reshape(PLANE, WIDE)
            table = disp[pl.ds(g * 4, 4)].reshape(4 * slots, PLANE)
            send[j, pl.ds(g * 4, 4)] = dot(table, lines).astype(BF16).reshape(4, slots, WIDE)

        each(pack, 0, 4)
        each(lambda o, j=j: slot_out(j, o).start())
        recv[j, z] = send[j, z]

    each(lambda o: zlab_in(o).wait_recv())
    flag_s[...] = jnp.broadcast_to(
        jnp.max(jnp.max(labr[:, 4:5, :].astype(F32), axis=0), axis=1, keepdims=True), (16, 128)
    ).astype(BF16)
    flag_copy().start()

    def interpolate(s):
        info = labr[s].astype(F32)
        member = info[0:1]
        plane, fraction = info[1:2], info[2:3] + jnp.where(member == 0.0, 0.5, 0.0)
        x = iota((EXTENT, 128), 0).astype(F32)
        away = x - (plane + fraction)
        t = away * (1.0 / EXTENT)
        t = t - jnp.round(t)
        t2 = t * t
        both = x + plane
        sign = 2.0 * (both - 2.0 * jnp.floor(both * 0.5)) - 1.0
        centred = fraction - 0.5
        lift = horner(COS_HALF, centred * centred) * (1.0 / EXTENT)
        value = sign * lift * horner(COS_HALF, t2) / (t * horner(SIN_HALF, t2))
        turned = value.T
        members = jnp.broadcast_to(member, (EXTENT, 128))
        members_turned = members.T
        for q in range(4):
            kern_t[q * EXTENT : (q + 1) * EXTENT, pl.ds(pl.multiple_of(s * 128, 128), 128)] = jnp.where(
                members == q + 1.0, value, 0.0
            ).astype(BF16)
            kern[s, :, q * EXTENT : (q + 1) * EXTENT] = jnp.where(
                members_turned == q + 1.0, turned, 0.0
            ).astype(BF16)
        focus[s] = jnp.broadcast_to(info[3:4] * 0.5, (128, 128)).T

    each(interpolate, 0, ZC)
    map_in().wait_recv()
    map_own().wait()

    lane = iota((1, WIDE), 1)
    column = lane - jnp.where(lane >= EXTENT, EXTENT, 0)
    column = jnp.where(column < EXTENT // 2, column, column - EXTENT).astype(F32)
    for j in range(CHUNKS):
        row = pen * (2 * CHUNKS) + 2 * j + jnp.where(lane >= EXTENT, 1, 0)
        row = jnp.where(row < EXTENT // 2, row, row - EXTENT).astype(F32)
        shell = (2.0 / EXTENT * row) ** 2 + (2.0 / EXTENT * column) ** 2
        each(lambda o, j=j: slot_in(j, o).wait_recv())

        def weigh(s, j=j, shell=shell):
            predicted = dot(kern[s, 0:slots, :], volume[j].reshape(4 * EXTENT, WIDE))
            half = focus[s, 0:slots, :]
            turns = jnp.concatenate([half, half], axis=1) * shell + PHASE
            r = turns - jnp.round(turns)
            wave = r * horner(SIN_TURN, r * r)
            value = -wave * (recv[j, s].astype(F32) + wave * predicted)
            weighted[pl.ds(pl.multiple_of(s * 128, 128), slots), :] = value.astype(BF16)

        each(weigh, 0, ZC)
        partial[j] = dot(kern_t[...], weighted[...]).reshape(2, 2 * EXTENT, WIDE)
        half_copy(j).start()
        half_copy(j).wait_recv()
        mine = partial[j, core] + partner[j]
        high, low = split(mine)
        along_z = []
        for yy in range(2):
            cut = slice(yy * EXTENT, (yy + 1) * EXTENT)
            along_z.append(dot(jnp.concatenate([high[:, cut], low[:, cut], high[:, cut]], axis=1), hz_ref[...]))
        high, low = split(jnp.concatenate(along_z, axis=1))
        pieces = []
        for c in range(2):
            cut = slice(c * EXTENT, (c + 1) * EXTENT)
            along_x = dot(hx_ref[...], jnp.concatenate([high[cut], low[cut], high[cut]], axis=0))
            pieces.append(along_x.reshape(PENS, 8, WIDE))
        fs[j] = jnp.concatenate(pieces, axis=1).astype(BF16)
        each(lambda o, j=j: cells_out(j, o).start())
        fr[j, pen] = fs[j, pen]

    for j in range(CHUNKS):
        each(lambda o, j=j: cells_in(j, o).wait_recv())

        def place(r, j=j):
            for yy in range(2):
                gather[r * 8 + 2 * j + yy] = fr[j, r, :, yy * EXTENT : (yy + 1) * EXTENT].astype(F32)

        each(place, 0, PENS)
    for pair in range(8):
        cells = jnp.concatenate([gather[:, 2 * pair, :], gather[:, 2 * pair + 1, :]], axis=1).astype(BF16)
        along_y = dot(hy_ref[...], jnp.concatenate([cells, cells], axis=0))
        for i in range(2):
            c, kx = divmod(2 * pair + i, 8)
            out_ref[c, kx] = along_y[:, i * EXTENT : (i + 1) * EXTENT]

    flag_copy().wait()
    most_ref[...] = jnp.maximum(flag_s[0:8].astype(F32), flag_r[0:8].astype(F32))
    map_out().wait_send()
    each(lambda o: lab_out(o).wait_send())
    each(lambda o: zlab_out(o).wait_send())
    for j in range(CHUNKS):
        half_copy(j).wait_send()
        each(lambda o, j=j: rows_out(j, o).wait_send())
        each(lambda o, j=j: slot_out(j, o).wait_send())
        each(lambda o, j=j: cells_out(j, o).wait_send())


def one_round(slots, first, collective, lab, slabs, maps, tables):
    dma = pltpu.SemaphoreType.DMA
    vmem = pl.BlockSpec(memory_space=pltpu.VMEM)
    anywhere = pl.BlockSpec(memory_space=pl.ANY)
    return pl.pallas_call(
        functools.partial(round_kernel, slots, first),
        out_shape=[
            jax.ShapeDtypeStruct((2, 8, EXTENT, EXTENT), F32),
            jax.ShapeDtypeStruct((8, 128), F32),
        ],
        in_specs=[vmem, anywhere, anywhere, vmem, vmem, vmem],
        out_specs=[vmem, vmem],
        scratch_shapes=[
            pltpu.VMEM((PENS, 16, 128), BF16),
            pltpu.VMEM((CHUNKS, PENS, PART, WIDE), BF16),
            pltpu.VMEM((ZC, slots, PLANE), BF16),
            pltpu.VMEM((ZC, 16, 128), BF16),
            pltpu.VMEM((ZC, 16, 128), BF16),
            pltpu.VMEM((CHUNKS, ZC, slots, WIDE), BF16),
            pltpu.VMEM((CHUNKS, ZC, slots, WIDE), BF16),
            pltpu.VMEM((CHUNKS, 4, EXTENT, WIDE), BF16),
            pltpu.VMEM((ZC, 128, 4 * EXTENT), BF16),
            pltpu.VMEM((4 * EXTENT, ZC * 128), BF16),
            pltpu.VMEM((ZC, 128, 128), F32),
            pltpu.VMEM((ZC * 128, WIDE), BF16),
            pltpu.VMEM((CHUNKS, 2, 2 * EXTENT, WIDE), F32),
            pltpu.VMEM((CHUNKS, 2 * EXTENT, WIDE), F32),
            pltpu.VMEM((CHUNKS, PENS, 16, WIDE), BF16),
            pltpu.VMEM((CHUNKS, PENS, 16, WIDE), BF16),
            pltpu.VMEM((EXTENT, 16, EXTENT), F32),
            pltpu.VMEM((16, 128), BF16),
            pltpu.VMEM((16, 128), BF16),
            dma((16,)), dma((16,)), dma((CHUNKS, 16)), dma((CHUNKS, 16)), dma((CHUNKS,)),
            dma, dma, dma, dma((16,)), dma((16,)), dma((CHUNKS, 16)), dma((CHUNKS, 16)),
            dma, dma, dma((CHUNKS,)), dma((CHUNKS,)), dma((CHUNKS, 16)), dma((CHUNKS, 16)),
        ],
        compiler_params=pltpu.CompilerParams(
            collective_id=collective, has_side_effects=True, vmem_limit_bytes=48 << 20
        ),
        name=f"round_{collective}",
    )(lab, slabs, maps, *tables)


def per_device(fourier_slabs, class_id, orientation, offset, tomogram, defocus, class_map):
    tomo_match = tomogram[None, :] == jnp.arange(defocus.shape[0], dtype=jnp.int32)[:, None]
    focus_here = jnp.sum(jnp.where(tomo_match, defocus.astype(F32)[:, None], 0.0), axis=0)
    fields = jnp.stack(
        [class_id[:, 0].astype(F32), orientation.astype(F32), offset.astype(F32), focus_here]
    )
    twice = jnp.concatenate([fields, fields], axis=1)
    side = jnp.arange(2 * PART, dtype=jnp.int32)[None, :] // PART
    lab = jnp.where(side == lax.rem(lax.axis_index("pen"), 2), twice, 0.0)
    lab = jnp.pad(lab, ((0, 12), (0, 0))).astype(BF16)
    slabs = fourier_slabs.reshape(PART, PENS * CHUNKS, WIDE).transpose(1, 0, 2)
    maps = class_map.reshape(2, EXTENT, CHUNKS, WIDE).transpose(2, 0, 1, 3)
    tables = [jnp.asarray(t) for t in hartley_tables()]
    gradient, most = one_round(MAIN, 0, 0, lab, slabs, maps, tables)
    return lax.cond(
        most[0, 0] > MAIN,
        lambda g: g + one_round(POOL - MAIN, MAIN, 1, lab, slabs, maps, tables)[0],
        lambda g: g,
        gradient,
    )


def solution(mesh):
    in_specs = (
        P(("cls", "pen"), None, None),
        P(("cls", "pen"), None),
        P(("cls", "pen")),
        P(("cls", "pen")),
        P(("cls", "pen")),
        P(),
        P("cls", None, "pen", None),
    )
    return jax.shard_map(
        per_device, mesh=mesh, in_specs=in_specs, out_specs=P("cls", "pen", None, None), check_vma=False
    )
```

time: 423 us -> 197 us (0.47); the launches traced: 415 us -> 197 us
  waiting for transfers between devices: 230 us -> 0 us
  Pallas kernels: 0 us -> 186 us
  matrix products: 53.7 us -> 0 us
  local copies, waits for them, and re-layouts: 45 us -> 6.96 us
  starting transfers between devices: 37.7 us -> 0 us
  blocking collectives: 26.5 us -> 0 us
  other arithmetic: 21.6 us -> 3.63 us
    all_to_all x4 -> x0, waiting for transfers between devices: 230 us -> none  [the longest x1 182 us: per_device(): lax.all_to_all(send_slabs, 'cls', split_axis=0, concat_axis=1, tiled=True)]
    pallas_call x0 -> x1, Pallas kernels: none -> 186 us  [one_round(): pl.pallas_call(functools.partial(round_kernel, slots, first), out_shape=[...]
    dot_general x7 -> x0, matrix products: 53.7 us -> none  [the longest x2 45 us: per_device(): jnp.dot(kernel, weighted, preferred_element_type=jnp.float32)]
    all_to_all x4 -> x0, starting transfers between devices: 37.7 us -> none  [the longest x1 16.7 us: per_device(): lax.all_to_all(send_labels, 'cls', split_axis=0, concat_axis=1, tiled=True)]
    all_to_all x1 -> x0, blocking collectives: 26.5 us -> none  [per_device(): lax.all_to_all(along_x, 'pen', split_axis=1, concat_axis=2, tiled=True)]
    all_to_all x4 -> x0, local copies, waits for them, and re-layouts: 16 us -> none  [the longest x2 7.91 us: per_device(): lax.all_to_all(lax.all_to_all(send_slabs, 'cls', split_axis=0, concat_axi...]
    convert_element_type x3 -> x0, local copies, waits for them, and re-layouts: 13.2 us -> none  [the longest x2 12.9 us: per_device(): slab_rows - contrast_map * predicted]
    convert_element_type x4 -> x2, other arithmetic: 9.75 us -> 1.31 us  [the longest x1 0.66 us: per_device(): class_id[:, 0].astype(F32)]
  transfers between devices with their start and end apart: 4 -> 0, of which waited for: 3 -> 0; matrix products, arithmetic and copies ran while one was open for 6% -> 0% of each run, Pallas kernels for 0% -> 0%
where the time goes in v1:
time: 197 us
  Pallas kernels  186 us (94%)
  local copies, waits for them, and re-layouts  6.96 us (4%)
  other arithmetic  3.63 us (2%)
    pallas_call x1, Pallas kernels, one_round(): pl.pallas_call(functools.partial(round_kernel, slots, first), out_shape=[...  186 us

profile of v1, /device:TPU:1, one launch (start us, length us, event | category | flops | bytes accessed | tf_op | source)
XLA Modules:
  0.0 197.1 jit_solution(4705839642996041906)
XLA Ops:
  0.0 0.7 convert_bitcast_fusion.1
  0.7 0.7 convert_bitcast_fusion
  1.3 0.7 convert_element_type.32
  2.0 0.8 select_reduce_fusion
  2.8 0.8 fusion
  3.6 1.4 copy.17
  5.0 0.2 copy.18
  5.3 2.7 %reshape.62 = bf16[64,64,256]{2,1,0:T(8,128)(2,1)S(1)} reshape(bf16[64,128,128]{2,1,0:T(8,128)(2,1)} %param.12) | data formatting | bytes 4194304 | tf_op jit(solution)/shard_map/reshape | solution.py:391
  7.9 0.0 copy-start
  7.9 0.0 copy-start.1
  8.0 0.0 copy-start.2
  8.0 1.2 copy.20
  9.2 0.0 copy-done
  9.2 0.0 copy-done.1
  9.2 0.0 copy-done.2
  9.2 185.6 %round_0.1 = (f32[2,8,128,128]{3,2,1,0:T(8,128)S(1)}, f32[8,128]{1,0:T(8,128)S(1)}) custom-call(bf16[16,128]{1,0:T(8,128)(2,1)S(1)} %pad.5.lab_ref, bf16[64,64,256]{2,1,0:T(8,128)(2,1)S(1)} %bitcast.15, bf16[4,2,128,256]{3,2,1,0:T(8,128)(2,1)S(1)} %bitcast.17, bf16[384,128]{1,0:T(8,128)(2,1)S(1)} %copy-done.1, bf16[128,384]{1,0:T(8,128)(2,1)S(1)} %copy-done, ...), custom_call_target="tpu_custom_call" | custom-call | tf_op jit(solution)/shard_map/round_0/pallas_call | solution.py:342
  194.8 0.5 slice.3
  196.0 0.2 conditional.1
  196.2 1.0 copy.24
  (2 shorter events, 0.0 us)
Async XLA Ops:
  7.9 1.2 copy-start
  7.9 1.2 copy-start.1
  8.0 1.2 copy-start.2

commit v2 on v1

v2 whole, which is shorter than its diff:
```python
import functools
import math

import jax
import jax.numpy as jnp
import numpy as np
from jax import lax
from jax.experimental import pallas as pl
from jax.experimental.pallas import tpu as pltpu
from jax.sharding import PartitionSpec as P

AMPLITUDE = 0.07
MESH = pl.DeviceIdType.MESH
F32 = jnp.float32
BF16 = jnp.bfloat16

EXTENT = 128
ZC = 16
PENS = 16
PART = 64
PLANE = PART * PENS
ROWS = 2
CHUNKS = 8 // ROWS
WIDE = ROWS * EXTENT
POOL = 128
MAIN = 96


def power_series(function, degree, reach):
    nodes = np.cos(np.pi * (np.arange(degree + 1) + 0.5) / (degree + 1))
    nodes = 0.5 * reach * (nodes + 1.0)
    return [float(c) for c in np.polyfit(nodes, function(nodes), degree)[::-1]]


SIN_TURN = power_series(lambda s: 2 * np.pi * np.sinc(2 * np.sqrt(s)), 6, 0.25)
SIN_HALF = power_series(lambda s: np.pi * np.sinc(np.sqrt(s)), 5, 0.25)
COS_HALF = power_series(lambda s: np.cos(np.pi * np.sqrt(s)), 5, 0.25)
PHASE = math.asin(AMPLITUDE) / (2 * math.pi)


def horner(coefficients, x):
    total = coefficients[-1]
    for c in coefficients[-2::-1]:
        total = total * x + c
    return total


def hartley_tables():
    k = np.arange(EXTENT)
    angles = 2.0 * np.pi / EXTENT * ((k[:, None] * k[None, :]) % EXTENT)
    table = ((np.cos(angles) + np.sin(angles)) / math.sqrt(EXTENT)).astype(np.float32)
    high = table.astype(jnp.bfloat16)
    low = (table - high.astype(np.float32)).astype(jnp.bfloat16)
    return (
        np.concatenate([high, high, low], 0),
        np.concatenate([high, high, low], 1),
        np.concatenate([high, low], 1),
    )


def iota(shape, dim):
    return lax.broadcasted_iota(jnp.int32, shape, dim)


def dot(a, b):
    return jnp.dot(a, b, preferred_element_type=F32)


def dot_nt(a, b):
    return lax.dot_general(a, b, (((1,), (1,)), ((), ())), preferred_element_type=F32)


def split(a):
    high = a.astype(BF16)
    return high, (a - high.astype(F32)).astype(BF16)


def abreast(parts):
    return parts[0] if len(parts) == 1 else jnp.concatenate(parts, axis=1)


def round_kernel(
    slots, first,
    ids_ref, plane_ref, offset_ref, tomo_ref, defocus_ref, slabs_ref, maps_ref, hz_ref, hx_ref, hy_ref,
    out_ref, most_ref,
    lab, labp, p1, disp, labs, labg, labr, send, recv, volume, kern, kern_t, focus, weighted,
    partial, partner, fs, fr, gather, flag_s, flag_r,
    lp_s, lp_r, p1_s, p1_r, own_s, cm_s, cm_r, cm_o, zl_s, zl_r, lb_s, lb_r, z_s, z_r, fl_s, fl_r, c_s, c_r, f_s, f_r,
):
    me = lax.axis_index("cls")
    pen = lax.axis_index("pen")
    z = me // 2
    core = lax.rem(me, 2)
    twin = (z * 2 + 1 - core, pen)

    def pen_at(o):
        return lax.rem(pen + o, PENS)

    def pen_from(o):
        return lax.rem(pen - o + PENS, PENS)

    def reach(i):
        half = (i + 1) // 2
        return lax.rem(half + lax.rem(i + 1, 2) * (ZC - 2 * half) + ZC, ZC)

    def chip_at(i):
        return lax.rem(z + reach(i), ZC)

    def chip_from(i):
        return lax.rem(z - reach(i) + ZC, ZC)

    def remote(src, dst, s, r, device):
        return pltpu.make_async_remote_copy(
            src_ref=src, dst_ref=dst, send_sem=s, recv_sem=r, device_id=device, device_id_type=MESH
        )

    def each(body, low=1, high=16):
        def step(i, carry):
            body(i)
            return carry

        lax.fori_loop(low, high, step, 0)

    barrier = pltpu.get_barrier_semaphore()

    def greet(o):
        pl.semaphore_signal(barrier, inc=1, device_id=(me, pen_at(o)), device_id_type=MESH)
        pl.semaphore_signal(barrier, inc=1, device_id=(chip_at(o) * 2 + core, pen), device_id_type=MESH)

    each(greet)
    pl.semaphore_signal(barrier, inc=1, device_id=twin, device_id_type=MESH)

    tomo_match = jnp.where(iota((256, PART), 0) == tomo_ref[...], 1.0, 0.0).astype(BF16)
    defocus = jnp.broadcast_to(defocus_ref[...].astype(F32), (8, 256)).astype(BF16)
    focus_here = dot(defocus, tomo_match)[0:1]
    line = iota((16, PART), 0)
    told = jnp.where(
        line == 0,
        ids_ref[...].astype(F32),
        jnp.where(
            line == 1,
            plane_ref[...].astype(F32),
            jnp.where(line == 2, offset_ref[...].astype(F32), jnp.where(line == 3, focus_here, 0.0)),
        ),
    )
    spot = iota((PART, 128), 0) + PART * lax.rem(pen, 2)
    spread = jnp.where(iota((PART, 128), 1) == spot, 1.0, 0.0).astype(BF16)
    lab[...] = dot(told.astype(BF16), spread).astype(BF16)
    labp[pen] = lab[...]
    labs[...] = jnp.zeros_like(labs)
    tri = jnp.where(iota((128, 128), 0) < iota((128, 128), 1), 1.0, 0.0).astype(BF16)

    pl.semaphore_wait(barrier, 31)

    def lab_out(o):
        return remote(lab, labp.at[pen], lp_s.at[o], lp_r.at[o], (me, pen_at(o)))

    def lab_in(o):
        return remote(lab, labp.at[pen_from(o)], lp_s.at[o], lp_r.at[o], (me, pen_at(o)))

    def rows_out(j, o):
        to = pen_at(o)
        return remote(slabs_ref.at[pl.ds(to * 8 + j * ROWS, ROWS)], p1.at[j, pen], p1_s.at[j, o], p1_r.at[j, o], (me, to))

    def rows_in(j, o):
        to = pen_at(o)
        return remote(slabs_ref.at[pl.ds(to * 8 + j * ROWS, ROWS)], p1.at[j, pen_from(o)], p1_s.at[j, o], p1_r.at[j, o], (me, to))

    def rows_own(j):
        return pltpu.make_async_copy(slabs_ref.at[pl.ds(pen * 8 + j * ROWS, ROWS)], p1.at[j, pen], own_s.at[j])

    def map_out():
        return remote(maps_ref, volume.at[:, pl.ds(2 * core, 2)], cm_s, cm_r, twin)

    def map_in():
        return remote(maps_ref, volume.at[:, pl.ds(2 - 2 * core, 2)], cm_s, cm_r, twin)

    def map_own():
        return pltpu.make_async_copy(maps_ref, volume.at[:, pl.ds(2 * core, 2)], cm_o)

    def zlab_out():
        o = lax.rem(pen - z + ZC, ZC)
        return remote(labs.at[pen], labg.at[z], zl_s, zl_r.at[o], (pen * 2 + core, pen))

    def zlab_in(o):
        source = lax.rem(z - o + ZC, ZC)
        return remote(labs.at[source], labg.at[source], zl_s, zl_r.at[o], (source * 2 + core, pen))

    def tell_out(o):
        return remote(labg, labr, lb_s.at[o], lb_r, (me, pen_at(o)))

    def tell_in():
        return remote(labg, labr, lb_s.at[0], lb_r, (me, z))

    def slot_out(j, i):
        to = chip_at(i)
        return remote(send.at[j, i], recv.at[j, i], z_s.at[j, i], z_r.at[j, i], (to * 2 + core, pen))

    def flag_copy():
        return remote(flag_s, flag_r, fl_s, fl_r, twin)

    def half_copy(j):
        return remote(partial.at[j, 1 - core], partner.at[j], c_s.at[j], c_r.at[j], twin)

    def cells_out(j, o):
        to = pen_at(o)
        return remote(fs.at[j, to], fr.at[j, pen], f_s.at[j, o], f_r.at[j, o], (me, to))

    def cells_in(j, o):
        to = pen_at(o)
        return remote(fs.at[j, to], fr.at[j, pen_from(o)], f_s.at[j, o], f_r.at[j, o], (me, to))

    def hand_out(j):
        each(lambda o: rows_out(j, o).start())
        rows_own(j).start()

    each(lambda o: lab_out(o).start())
    hand_out(0)
    hand_out(1)

    each(lambda o: lab_in(o).wait_recv())
    fields = jnp.concatenate(
        [labp[2 * i].astype(F32) + labp[2 * i + 1].astype(F32) for i in range(PENS // 2)], axis=1
    )
    ids = fields[0:1]
    chip = jnp.floor(ids * 0.25)
    local = ids - 4.0 * chip + 1.0
    running = jnp.zeros((ZC, 1), F32)
    ranks = []
    for i in range(PLANE // 128):
        part = chip[:, i * 128 : (i + 1) * 128]
        hot = jnp.where(iota((ZC, 128), 0).astype(F32) == part, 1.0, 0.0)
        before = dot(hot.astype(BF16), tri) + running
        ranks.append(jnp.sum(hot * before, axis=0, keepdims=True))
        running = running + jnp.sum(hot, axis=1, keepdims=True)
    most = jnp.max(running, axis=0, keepdims=True)
    rank = jnp.concatenate(ranks, axis=1) - float(first)
    rank = jnp.where((rank >= 0.0) & (rank < float(slots)), rank, -1.0)
    described = jnp.where(iota((16, PLANE), 0) == 0, local, fields).astype(BF16)
    row_of = iota((slots, PLANE), 0).astype(F32)

    def assign(d):
        here = jnp.where(chip == d.astype(F32), rank, -1.0)
        disp[d] = jnp.where(row_of == here, 1.0, 0.0).astype(BF16)

    def describe(d):
        held = dot_nt(described, disp[d])
        labs[d, :, 0:slots] = jnp.where(iota((16, slots), 0) == 4, most, held).astype(BF16)

    def pack(j):
        each(lambda o: rows_in(j, o).wait_recv())
        rows_own(j).wait()

        def some(g):
            table = jnp.concatenate([disp[chip_at(4 * g + k)] for k in range(4)], axis=0)
            lines = abreast([p1[j, :, r].reshape(PLANE, EXTENT) for r in range(ROWS)])
            send[j, pl.ds(g * 4, 4)] = dot(table, lines).astype(BF16).reshape(4, slots, WIDE)
            each(lambda i: slot_out(j, i).start(), jnp.maximum(4 * g, 1), 4 * g + 4)

        each(some, 0, 4)
        recv[j, 0] = send[j, 0]

    each(assign, 0, ZC)
    pack(0)
    each(hand_out, 2, min(4, CHUNKS))
    pack(1)
    each(describe, 0, ZC)

    @pl.when(pen != z)
    def _():
        zlab_out().start()

    map_out().start()
    map_own().start()
    each(hand_out, 4, CHUNKS)
    each(pack, 2, CHUNKS)

    @pl.when(pen == z)
    def _():
        labg[z] = labs[z]
        each(lambda o: zlab_in(o).wait_recv())
        each(lambda o: tell_out(o).start())
        labr[...] = labg[...]

    @pl.when(pen != z)
    def _():
        tell_in().wait_recv()

    flag_s[...] = jnp.broadcast_to(
        jnp.max(jnp.max(labr[:, 4:5, :].astype(F32), axis=0), axis=1, keepdims=True), (16, 128)
    ).astype(BF16)
    flag_copy().start()

    def interpolate(g):
        for k in range(4):
            i = 4 * g + k
            info = labr[chip_from(i)].astype(F32)
            member = info[0:1]
            plane, fraction = info[1:2], info[2:3] + jnp.where(member == 0.0, 0.5, 0.0)
            x = iota((EXTENT, 128), 0).astype(F32)
            away = x - (plane + fraction)
            t = away * (1.0 / EXTENT)
            t = t - jnp.round(t)
            t2 = t * t
            both = x + plane
            sign = 2.0 * (both - 2.0 * jnp.floor(both * 0.5)) - 1.0
            centred = fraction - 0.5
            lift = horner(COS_HALF, centred * centred) * (1.0 / EXTENT)
            value = sign * lift * horner(COS_HALF, t2) / (t * horner(SIN_HALF, t2))
            turned = value.T
            members = jnp.broadcast_to(member, (EXTENT, 128))
            members_turned = members.T
            for q in range(4):
                cut = slice(q * EXTENT, (q + 1) * EXTENT)
                kern_t[g, cut, k * 128 : (k + 1) * 128] = jnp.where(members == q + 1.0, value, 0.0).astype(BF16)
                kern[i, :, cut] = jnp.where(members_turned == q + 1.0, turned, 0.0).astype(BF16)
            focus[i] = jnp.broadcast_to(info[3:4] * 0.5, (128, 128)).T

    each(interpolate, 0, 4)
    weighted[...] = jnp.zeros_like(weighted)
    map_in().wait_recv()
    map_own().wait()

    column = iota((1, EXTENT), 1)
    column = jnp.where(column < EXTENT // 2, column, column - EXTENT).astype(F32)

    def place(j):
        each(lambda o: cells_in(j, o).wait_recv())

        def one(r):
            for k in range(ROWS):
                gather[r * 8 + j * ROWS + k] = fr[j, r, :, k * EXTENT : (k + 1) * EXTENT].astype(F32)

        each(one, 0, PENS)

    def work(j):
        shells = []
        for k in range(ROWS):
            row = jnp.full((1, EXTENT), pen * 8 + j * ROWS + k, jnp.int32)
            row = jnp.where(row < EXTENT // 2, row, row - EXTENT).astype(F32)
            shells.append((2.0 / EXTENT * row) ** 2 + (2.0 / EXTENT * column) ** 2)
        shell = abreast(shells)

        def weigh(i):
            @pl.when(i > 0)
            def _():
                slot_out(j, i).wait_recv()

            maps = abreast([volume[j * ROWS + k].reshape(4 * EXTENT, EXTENT) for k in range(ROWS)])
            predicted = dot(kern[i, 0:slots, :], maps)
            turns = abreast([focus[i, 0:slots, :]] * ROWS) * shell + PHASE
            r = turns - jnp.round(turns)
            wave = r * horner(SIN_TURN, r * r)
            value = -wave * (recv[j, i].astype(F32) + wave * predicted)
            weighted[pl.ds(pl.multiple_of(i * 128, 128), slots), :] = value.astype(BF16)

        total = None
        for g in range(4):
            each(weigh, 4 * g, 4 * g + 4)
            term = dot(kern_t[g], weighted[g * 512 : (g + 1) * 512, :])
            total = term if total is None else total + term
        partial[j] = total.reshape(2, 2 * EXTENT, WIDE)
        half_copy(j).start()

        @pl.when(j > 0)
        def _():
            finish(j - 1)

        @pl.when(j > 1)
        def _():
            place(j - 2)

    def finish(j):
        half_copy(j).wait_recv()
        mine = partial[j, core] + partner[j]
        high, low = split(mine)
        along_z = []
        for k in range(ROWS):
            cut = slice(k * EXTENT, (k + 1) * EXTENT)
            along_z.append(dot(abreast([high[:, cut], low[:, cut], high[:, cut]]), hz_ref[...]))
        high, low = split(abreast(along_z))
        pieces = []
        for c in range(2):
            cut = slice(c * EXTENT, (c + 1) * EXTENT)
            along_x = dot(hx_ref[...], jnp.concatenate([high[cut], low[cut], high[cut]], axis=0))
            pieces.append(along_x.reshape(PENS, 8, WIDE))
        fs[j] = jnp.concatenate(pieces, axis=1).astype(BF16)
        each(lambda o: cells_out(j, o).start())
        fr[j, pen] = fs[j, pen]

    each(work, 0, CHUNKS)
    finish(CHUNKS - 1)
    place(CHUNKS - 2)
    place(CHUNKS - 1)
    for pair in range(8):
        cells = jnp.concatenate([gather[:, 2 * pair, :], gather[:, 2 * pair + 1, :]], axis=1).astype(BF16)
        along_y = dot(hy_ref[...], jnp.concatenate([cells, cells], axis=0))
        for i in range(2):
            c, kx = divmod(2 * pair + i, 8)
            out_ref[c, kx] = along_y[:, i * EXTENT : (i + 1) * EXTENT]

    flag_copy().wait()
    most_ref[...] = jnp.maximum(flag_s[0:8].astype(F32), flag_r[0:8].astype(F32))
    map_out().wait_send()
    each(lambda o: lab_out(o).wait_send())

    @pl.when(pen != z)
    def _():
        zlab_out().wait_send()

    @pl.when(pen == z)
    def _():
        each(lambda o: tell_out(o).wait_send())

    def drain(j):
        half_copy(j).wait_send()
        each(lambda o: rows_out(j, o).wait_send())
        each(lambda i: slot_out(j, i).wait_send())
        each(lambda o: cells_out(j, o).wait_send())

    each(drain, 0, CHUNKS)


def one_round(slots, first, collective, operands, tables):
    dma = pltpu.SemaphoreType.DMA
    vmem = pl.BlockSpec(memory_space=pltpu.VMEM)
    anywhere = pl.BlockSpec(memory_space=pl.ANY)
    return pl.pallas_call(
        functools.partial(round_kernel, slots, first),
        out_shape=[
            jax.ShapeDtypeStruct((2, 8, EXTENT, EXTENT), F32),
            jax.ShapeDtypeStruct((8, 128), F32),
        ],
        in_specs=[vmem] * 5 + [anywhere] * 2 + [vmem] * 3,
        out_specs=[vmem, vmem],
        scratch_shapes=[
            pltpu.VMEM((16, 128), BF16),
            pltpu.VMEM((PENS, 16, 128), BF16),
            pltpu.VMEM((CHUNKS, PENS, ROWS, PART, EXTENT), BF16),
            pltpu.VMEM((ZC, slots, PLANE), BF16),
            pltpu.VMEM((ZC, 16, 128), BF16),
            pltpu.VMEM((ZC, 16, 128), BF16),
            pltpu.VMEM((ZC, 16, 128), BF16),
            pltpu.VMEM((CHUNKS, ZC, slots, WIDE), BF16),
            pltpu.VMEM((CHUNKS, ZC, slots, WIDE), BF16),
            pltpu.VMEM((8, 4, EXTENT, EXTENT), BF16),
            pltpu.VMEM((ZC, 128, 4 * EXTENT), BF16),
            pltpu.VMEM((4, 4 * EXTENT, 512), BF16),
            pltpu.VMEM((ZC, 128, 128), F32),
            pltpu.VMEM((ZC * 128, WIDE), BF16),
            pltpu.VMEM((CHUNKS, 2, 2 * EXTENT, WIDE), F32),
            pltpu.VMEM((CHUNKS, 2 * EXTENT, WIDE), F32),
            pltpu.VMEM((CHUNKS, PENS, 16, WIDE), BF16),
            pltpu.VMEM((CHUNKS, PENS, 16, WIDE), BF16),
            pltpu.VMEM((EXTENT, 16, EXTENT), F32),
            pltpu.VMEM((16, 128), BF16),
            pltpu.VMEM((16, 128), BF16),
            dma((16,)), dma((16,)), dma((CHUNKS, 16)), dma((CHUNKS, 16)), dma((CHUNKS,)),
            dma, dma, dma, dma, dma((16,)), dma((16,)), dma, dma((CHUNKS, 16)), dma((CHUNKS, 16)),
            dma, dma, dma((CHUNKS,)), dma((CHUNKS,)), dma((CHUNKS, 16)), dma((CHUNKS, 16)),
        ],
        compiler_params=pltpu.CompilerParams(
            collective_id=collective, has_side_effects=True, vmem_limit_bytes=48 << 20
        ),
        name=f"round_{collective}",
    )(*operands, *tables)


def per_device(fourier_slabs, class_id, orientation, offset, tomogram, defocus, class_map):
    operands = [
        class_id.reshape(1, PART),
        orientation.reshape(1, PART),
        offset.reshape(1, PART),
        tomogram.reshape(1, PART),
        defocus.reshape(1, 256),
        fourier_slabs.transpose(1, 0, 2),
        class_map.transpose(2, 0, 1, 3),
    ]
    tables = [jnp.asarray(t) for t in hartley_tables()]
    gradient, most = one_round(MAIN, 0, 0, operands, tables)
    return lax.cond(
        most[0, 0] > MAIN,
        lambda g: g + one_round(POOL - MAIN, MAIN, 1, operands, tables)[0],
        lambda g: g,
        gradient,
    )


def solution(mesh):
    in_specs = (
        P(("cls", "pen"), None, None),
        P(("cls", "pen"), None),
        P(("cls", "pen")),
        P(("cls", "pen")),
        P(("cls", "pen")),
        P(),
        P("cls", None, "pen", None),
    )
    return jax.shard_map(
        per_device, mesh=mesh, in_specs=in_specs, out_specs=P("cls", "pen", None, None), check_vma=False
    )
```

time: 197 us -> 281 us (1.43)
  Pallas kernels: 186 us -> 273 us
  other arithmetic: 3.63 us -> 0.29 us
    pallas_call x1 -> x2, Pallas kernels: 186 us -> 273 us  [one_round(): pl.pallas_call(functools.partial(round_kernel, slots, first), out_shape=[...]
    reshape x3 -> x1, local copies, waits for them, and re-layouts: 4.07 us -> 0.66 us  [per_device(): defocus.reshape(1, 256)]
    unnamed x8 -> x17, local copies, waits for them, and re-layouts: 2.37 us -> 5.2 us
where the time goes in v2:
time: 281 us; the launch traced here: 280 us
  Pallas kernels  273 us (97%)
  local copies, waits for them, and re-layouts  6.37 us (2%)
    pallas_call x2, Pallas kernels, one_round(): pl.pallas_call(functools.partial(round_kernel, slots, first), out_shape=[...  273 us

profile of v2, /device:TPU:1, one launch (start us, length us, event | category | flops | bytes accessed | tf_op | source)
XLA Modules:
  0.0 280.5 jit_solution(17995439475315807265)
XLA Ops:
  0.0 0.7 reshape.23.defocus_ref
  0.7 1.1 copy.18
  1.8 0.0 copy-start
  1.8 0.0 copy-start.1
  1.8 0.0 copy-start.2
  1.8 0.0 copy-start.3
  1.9 0.0 copy-start.4
  1.9 0.0 copy-start.5
  1.9 0.0 copy-start.6
  1.9 3.0 %copy.17 = bf16[64,128,128]{2,0,1:T(8,128)(2,1)S(1)} copy(bf16[64,128,128]{2,1,0:T(8,128)(2,1)} %param.12) | data formatting | bytes 4194304 | tf_op args[0]
  4.9 0.0 copy-done
  4.9 0.0 copy-done.1
  5.0 0.0 copy-done.2
  5.0 0.0 copy-done.3
  5.0 0.0 copy-done.4
  5.0 0.0 copy-done.5
  5.0 0.0 copy-done.6
  5.0 180.6 %round_0.1 = (f32[2,8,128,128]{3,2,1,0:T(8,128)S(1)}, f32[8,128]{1,0:T(8,128)S(1)}) custom-call(s32[1,64]{1,0:T(1,128)S(1)} %bitcast.15, s32[1,64]{1,0:T(1,128)S(1)} %bitcast.17, bf16[1,64]{1,0:T(2,128)(2,1)S(1)} %bitcast.19, s32[1,64]{1,0:T(1,128)S(1)} %bitcast.21, bf16[1,256]{1,0:T(2,128)(2,1)S(1)} %reshape.23.defocus_ref, ...), custom_call_target="tpu_custom_call" | custom-call | tf_op jit(solution)/shard_map/round_0/pallas_call | solution.py:428
  185.7 0.5 slice.3
  186.8 92.7 %conditional.1 = (f32[2,8,128,128]{3,2,1,0:T(8,128)S(1)}) conditional(s32[]{:T(128)} %bitcast.6, f32[2,8,128,128]{3,2,1,0:T(8,128)S(1)} %get-tuple-element.46, (s32[1,64]{1,0:T(1,128)S(1)}, s32[1,64]{1,0:T(1,128)S(1)}, bf16[1,64]{1,0:T(2,128)(2,1)S(1)}, s32[1,64]{1,0:T(1,128)S(1)}, bf16[1,256]{1,0:T(2,128)(2,1)S(1)}, ...), branch_computations={%region_0.0_spmd, %region_1.0_spmd} | conditional | flops 262144 | bytes 3145736 | solution.py:481
  186.8 92.4 %round_1.1 = (f32[2,8,128,128]{3,2,1,0:T(8,128)S(1)}, f32[8,128]{1,0:T(8,128)}) custom-call(s32[1,64]{1,0:T(1,128)S(1)} %get-tuple-element.32.ids_ref, s32[1,64]{1,0:T(1,128)S(1)} %get-tuple-element.33.plane_ref, bf16[1,64]{1,0:T(2,128)(2,1)S(1)} %get-tuple-element.34.offset_ref, s32[1,64]{1,0:T(1,128)S(1)} %get-tuple-element.35.tomo_ref, ...), custom_call_target="tpu_custom_call" | custom-call | tf_op jit(solution)/shard_map/cond/branch_1_fun/round_1/pallas_call | solution.py:428
  279.2 0.3 add.2
  279.5 1.0 copy.22
Async XLA Ops:
  1.8 3.1 %copy-start = (bf16[128,384]{1,0:T(8,128)(2,1)S(1)}, bf16[128,384]{1,0:T(8,128)(2,1)}, u32[]{:S(2)}) copy-start(bf16[128,384]{1,0:T(8,128)(2,1)} %constant.10.clone.hx_ref) | copy-start | bytes 294916
  1.8 3.1 %copy-start.1 = (bf16[384,128]{1,0:T(8,128)(2,1)S(1)}, bf16[384,128]{1,0:T(8,128)(2,1)}, u32[]{:S(2)}) copy-start(bf16[384,128]{1,0:T(8,128)(2,1)} %constant.9.clone.hz_ref) | copy-start | bytes 294916
  1.8 3.1 %copy-start.2 = (bf16[128,256]{1,0:T(8,128)(2,1)S(1)}, bf16[128,256]{1,0:T(8,128)(2,1)}, u32[]{:S(2)}) copy-start(bf16[128,256]{1,0:T(8,128)(2,1)} %constant.11.clone.hy_ref) | copy-start | bytes 196612
  1.8 3.1 %copy-start.3 = (s32[64,1]{0,1:T(1,128)S(1)}, s32[64,1]{0,1:T(1,128)}, u32[]{:S(2)}) copy-start(s32[64,1]{0,1:T(1,128)} %param.13) | copy-start | bytes 772
  1.9 3.1 %copy-start.4 = (s32[64]{0:T(128)S(1)}, s32[64]{0:T(128)}, u32[]{:S(2)}) copy-start(s32[64]{0:T(128)} %param.14) | copy-start | bytes 772
  1.9 3.1 %copy-start.5 = (bf16[64]{0:T(256)(128)(2,1)S(1)}, bf16[64]{0:T(256)(128)(2,1)}, u32[]{:S(2)}) copy-start(bf16[64]{0:T(256)(128)(2,1)} %param.15) | copy-start | bytes 388
  1.9 3.1 %copy-start.6 = (s32[64]{0:T(128)S(1)}, s32[64]{0:T(128)}, u32[]{:S(2)}) copy-start(s32[64]{0:T(128)} %param.16) | copy-start | bytes 772
